TPU v7x, 32 devices: a whole 2x2x4 slice. The times are simulated.
32 devices in a mesh: dp: 8 (over y, x, core), seq: 4 (over z).
Axes of the slice: x: 2, y: 2, z: 4, core: 2. Of those that a mesh axis runs over, the one named last changes fastest.
Arguments:
- tokens: bfloat16 [16, 1024, 512], P('dp', 'seq'), may hold values from -6 to 6
- memory: bfloat16 [16, 1024, 512], P('dp', 'seq'), may hold values from -6 to 6
- tgt_segments: int32 [16, 1024], P('dp'), may hold values from 0 to 2, as said below
- mem_segments: int32 [16, 1024], P('dp'), may hold values from 0 to 2, as said below
- cotangent: bfloat16 [16, 1024, 512], P('dp', 'seq'), may hold values from -6 to 6
- w_qkv: bfloat16 [512, 1536], replicated, may hold values from -0.25 to 0.25
- w_self_out: bfloat16 [512, 512], replicated, may hold values from -1.5 to 1.5
- w_cross_q: bfloat16 [512, 512], replicated, may hold values from -0.25 to 0.25
- w_cross_kv: bfloat16 [512, 1024], replicated, may hold values from -0.25 to 0.25
- w_cross_out: bfloat16 [512, 512], replicated, may hold values from -1.5 to 1.5
- w_up: bfloat16 [512, 2048], replicated, may hold values from -0.25 to 0.25
- w_down: bfloat16 [2048, 512], replicated, may hold values from -0.125 to 0.125
- ln1_gain: float32 [512], replicated, may hold values from 0.25 to 1.75
- ln1_bias: float32 [512], replicated, may hold values from -1.8 to 1.8
- ln2_gain: float32 [512], replicated, may hold values from 0.25 to 1.75
- ln2_bias: float32 [512], replicated, may hold values from -1.8 to 1.8
- ln3_gain: float32 [512], replicated, may hold values from 0.25 to 1.75
- ln3_bias: float32 [512], replicated, may hold values from -1.8 to 1.8
Outputs:
- output: bfloat16 [16, 1024, 512], P('dp', 'seq')
- grad_tokens: float32 [16, 1024, 512], P('dp', 'seq')
- grad_memory: float32 [16, 1024, 512], P('dp', 'seq')
- grad_w_qkv: float32 [512, 1536], replicated
- grad_w_self_out: float32 [512, 512], replicated
- grad_w_cross_q: float32 [512, 512], replicated
- grad_w_cross_kv: float32 [512, 1024], replicated
- grad_w_cross_out: float32 [512, 512], replicated
- grad_w_up: float32 [512, 2048], replicated
- grad_w_down: float32 [2048, 512], replicated
- grad_ln1_gain: float32 [512], replicated
- grad_ln1_bias: float32 [512], replicated
- grad_ln2_gain: float32 [512], replicated
- grad_ln2_bias: float32 [512], replicated
- grad_ln3_gain: float32 [512], replicated
- grad_ln3_bias: float32 [512], replicated
Inputs may be any that keep to these rules, and one draw needn't show every extreme that they name: `tgt_segments`: along a row the ids never fall and all three occur; document 1 begins within the row's first 256 positions and ends within its last 256. `mem_segments`: along a row the ids never fall and all three occur.
All inputs are finite; a program needn't handle non-finite values.
Results may differ from a plain program's by a relative error of at most 0.02.
Values may be sent and summed in bfloat16 or wider, within the bound.
No kernel may reach another device: no remote copies, remote signals or barrier semaphores. Data moves between devices by JAX's collectives and lax.ppermute only.
A program may use at most 128 MiB of HBM per device.

v0:
```python
import math
import jax
import jax.numpy as jnp
from jax import lax
from jax.sharding import PartitionSpec as P

HEAD_DIM = 64


def mat_dot(left, right):
    return jnp.dot(left, right, preferred_element_type=jnp.float32)


def left_dot(left, right):
    return lax.dot_general(
        left, right, (((0,), (0,)), ((), ())), preferred_element_type=jnp.float32
    )


def right_dot(left, right):
    return lax.dot_general(
        left, right, (((1,), (1,)), ((), ())), preferred_element_type=jnp.float32
    )


def layer_norm(values, gain, bias):
    centre = values - jnp.mean(values, axis=-1, keepdims=True)
    recip = lax.rsqrt(jnp.mean(centre * centre, axis=-1, keepdims=True) + 1e-05)
    normed = centre * recip
    return (normed * gain + bias, normed, recip)


def norm_back(grad_out, normed, recip, gain):
    grad_gain = jnp.sum(grad_out * normed, axis=0)
    grad_bias = jnp.sum(grad_out, axis=0)
    scaled = grad_out * gain
    grad_in = recip * (
        scaled
        - jnp.mean(scaled, axis=-1, keepdims=True)
        - normed * jnp.mean(scaled * normed, axis=-1, keepdims=True)
    )
    return (grad_in, grad_gain, grad_bias)


def causal_mask(segment_row):
    place = jnp.arange(segment_row.shape[0])
    return (place[None, :] <= place[:, None]) & (segment_row[:, None] == segment_row[None, :])


def cross_mask(tgt_row, mem_row):
    return tgt_row[:, None] == mem_row[None, :]


def masked_scores(queries, key_heads, allowed, score_scale):
    scores = (
        jnp.einsum("qhd,khd->hqk", queries, key_heads, preferred_element_type=jnp.float32)
        * score_scale
    )
    return jnp.where(allowed[None], scores, -1000000000.0)


def attend_forward(queries, key_heads, value_heads, allowed, score_scale):
    scores = masked_scores(queries, key_heads, allowed, score_scale)
    highest = jnp.max(scores, axis=-1, keepdims=True)
    expo = jnp.exp(scores - highest)
    total = jnp.sum(expo, axis=-1, keepdims=True)
    probs = (expo / total).astype(jnp.bfloat16)
    context = jnp.einsum("hqk,khd->qhd", probs, value_heads, preferred_element_type=jnp.float32)
    return (context.astype(jnp.bfloat16), highest + jnp.log(total))


def attend_backward(queries, key_heads, value_heads, log_total, d_context, allowed, score_scale):
    scores = masked_scores(queries, key_heads, allowed, score_scale)
    probs = jnp.exp(scores - log_total)
    d_values = jnp.einsum(
        "hqk,qhd->khd", probs.astype(jnp.bfloat16), d_context, preferred_element_type=jnp.float32
    ).astype(jnp.bfloat16)
    d_probs = jnp.einsum("qhd,khd->hqk", d_context, value_heads, preferred_element_type=jnp.float32)
    centre = jnp.sum(probs * d_probs, axis=-1, keepdims=True)
    d_scores = (probs * (d_probs - centre)).astype(jnp.bfloat16)
    d_queries = (
        jnp.einsum("hqk,khd->qhd", d_scores, key_heads, preferred_element_type=jnp.float32)
        * score_scale
    ).astype(jnp.bfloat16)
    d_keys = (
        jnp.einsum("hqk,qhd->khd", d_scores, queries, preferred_element_type=jnp.float32)
        * score_scale
    ).astype(jnp.bfloat16)
    return (d_queries, d_keys, d_values)


def body(
    tokens,
    memory,
    tgt_segments,
    mem_segments,
    cotangent,
    w_qkv,
    w_self_out,
    w_cross_q,
    w_cross_kv,
    w_cross_out,
    w_up,
    w_down,
    ln1_gain,
    ln1_bias,
    ln2_gain,
    ln2_bias,
    ln3_gain,
    ln3_bias,
):
    row_count, tok_local, model_width = tokens.shape
    mem_local = memory.shape[1]
    seq_parts = lax.axis_size("seq")
    head_share = model_width // seq_parts
    heads_here = head_share // HEAD_DIM
    seq_len = tgt_segments.shape[1]
    mem_len = mem_segments.shape[1]
    score_scale = 1.0 / math.sqrt(HEAD_DIM)
    token_total = row_count * tok_local
    flat_tokens = tokens.reshape(token_total, model_width)
    flat_memory = memory.reshape(row_count * mem_local, model_width)
    mixed_proj = (
        mat_dot(flat_tokens, w_qkv)
        .astype(jnp.bfloat16)
        .reshape(row_count, tok_local, 3, seq_parts, head_share)
    )
    self_heads = lax.all_to_all(mixed_proj, "seq", split_axis=3, concat_axis=1, tiled=True).reshape(
        row_count, seq_len, 3, heads_here, HEAD_DIM
    )
    memory_proj = (
        mat_dot(flat_memory, w_cross_kv)
        .astype(jnp.bfloat16)
        .reshape(row_count, mem_local, 2, seq_parts, head_share)
    )
    memory_heads = lax.all_to_all(
        memory_proj, "seq", split_axis=3, concat_axis=1, tiled=True
    ).reshape(row_count, mem_len, 2, heads_here, HEAD_DIM)
    self_q = self_heads[:, :, 0]
    self_k = self_heads[:, :, 1]
    self_v = self_heads[:, :, 2]
    memory_k = memory_heads[:, :, 0]
    memory_v = memory_heads[:, :, 1]

    def self_forward(row_item):
        queries, key_heads, value_heads, segment_row = row_item
        return attend_forward(
            queries, key_heads, value_heads, causal_mask(segment_row), score_scale
        )

    self_context, self_lse = lax.map(self_forward, (self_q, self_k, self_v, tgt_segments))
    self_back = lax.all_to_all(
        self_context.reshape(row_count, seq_len, 1, head_share),
        "seq",
        split_axis=1,
        concat_axis=2,
        tiled=True,
    )
    context_one = self_back.reshape(token_total, model_width)
    attn_one = mat_dot(context_one, w_self_out)
    norm_one, normed_one, recip_one = layer_norm(
        flat_tokens.astype(jnp.float32) + attn_one, ln1_gain, ln1_bias
    )
    norm_one_low = norm_one.astype(jnp.bfloat16)
    cross_proj = (
        mat_dot(norm_one_low, w_cross_q)
        .astype(jnp.bfloat16)
        .reshape(row_count, tok_local, 1, seq_parts, head_share)
    )
    cross_q = lax.all_to_all(cross_proj, "seq", split_axis=3, concat_axis=1, tiled=True).reshape(
        row_count, seq_len, heads_here, HEAD_DIM
    )

    def cross_forward(row_item):
        queries, key_heads, value_heads, tgt_row, mem_row = row_item
        return attend_forward(
            queries, key_heads, value_heads, cross_mask(tgt_row, mem_row), score_scale
        )

    cross_context, cross_lse = lax.map(
        cross_forward, (cross_q, memory_k, memory_v, tgt_segments, mem_segments)
    )
    cross_back = lax.all_to_all(
        cross_context.reshape(row_count, seq_len, 1, head_share),
        "seq",
        split_axis=1,
        concat_axis=2,
        tiled=True,
    )
    context_two = cross_back.reshape(token_total, model_width)
    attn_two = mat_dot(context_two, w_cross_out)
    norm_two, normed_two, recip_two = layer_norm(norm_one + attn_two, ln2_gain, ln2_bias)
    norm_two_low = norm_two.astype(jnp.bfloat16)
    pre_act = mat_dot(norm_two_low, w_up)
    sigma = jax.nn.sigmoid(pre_act)
    hidden_low = (pre_act * sigma).astype(jnp.bfloat16)
    fed = mat_dot(hidden_low, w_down)
    result, normed_three, recip_three = layer_norm(norm_two + fed, ln3_gain, ln3_bias)
    output = result.astype(jnp.bfloat16).reshape(row_count, tok_local, model_width)
    grad_out = cotangent.reshape(token_total, model_width).astype(jnp.float32)
    d_resid_three, d_gain_three, d_bias_three = norm_back(
        grad_out, normed_three, recip_three, ln3_gain
    )
    d_fed_low = d_resid_three.astype(jnp.bfloat16)
    grad_down = left_dot(hidden_low, d_fed_low)
    d_hidden = right_dot(d_fed_low, w_down)
    d_pre_low = (d_hidden * sigma * (1.0 + pre_act * (1.0 - sigma))).astype(jnp.bfloat16)
    grad_up = left_dot(norm_two_low, d_pre_low)
    d_norm_two = d_resid_three + right_dot(d_pre_low, w_up)
    d_resid_two, d_gain_two, d_bias_two = norm_back(d_norm_two, normed_two, recip_two, ln2_gain)
    d_attn_two = d_resid_two.astype(jnp.bfloat16)
    grad_cross_out = left_dot(context_two, d_attn_two)
    d_context_two = (
        right_dot(d_attn_two, w_cross_out)
        .astype(jnp.bfloat16)
        .reshape(row_count, tok_local, seq_parts, head_share)
    )
    d_cross_heads = lax.all_to_all(
        d_context_two, "seq", split_axis=2, concat_axis=1, tiled=True
    ).reshape(row_count, seq_len, heads_here, HEAD_DIM)

    def cross_backward(row_item):
        queries, key_heads, value_heads, log_total, d_context, tgt_row, mem_row = row_item
        return attend_backward(
            queries,
            key_heads,
            value_heads,
            log_total,
            d_context,
            cross_mask(tgt_row, mem_row),
            score_scale,
        )

    d_cross_q, d_mem_keys, d_mem_values = lax.map(
        cross_backward,
        (cross_q, memory_k, memory_v, cross_lse, d_cross_heads, tgt_segments, mem_segments),
    )
    d_memory_kv = jnp.stack((d_mem_keys, d_mem_values), axis=2).reshape(
        row_count, mem_len, 2, 1, head_share
    )
    back_query, back_memory = (
        lax.all_to_all(
            d_cross_q.reshape(row_count, seq_len, 1, 1, head_share),
            "seq",
            split_axis=1,
            concat_axis=3,
            tiled=True,
        ),
        lax.all_to_all(d_memory_kv, "seq", split_axis=1, concat_axis=3, tiled=True),
    )
    d_query_flat = back_query.reshape(token_total, model_width)
    d_memory_flat = back_memory.reshape(row_count * mem_local, 2 * model_width)
    grad_cross_q = left_dot(norm_one_low, d_query_flat)
    grad_cross_kv = left_dot(flat_memory, d_memory_flat)
    grad_memory = right_dot(d_memory_flat, w_cross_kv).reshape(row_count, mem_local, model_width)
    d_norm_one = d_resid_two + right_dot(d_query_flat, w_cross_q)
    d_resid_one, d_gain_one, d_bias_one = norm_back(d_norm_one, normed_one, recip_one, ln1_gain)
    d_attn_one = d_resid_one.astype(jnp.bfloat16)
    grad_self_out = left_dot(context_one, d_attn_one)
    d_context_one = (
        right_dot(d_attn_one, w_self_out)
        .astype(jnp.bfloat16)
        .reshape(row_count, tok_local, seq_parts, head_share)
    )
    d_self_heads = lax.all_to_all(
        d_context_one, "seq", split_axis=2, concat_axis=1, tiled=True
    ).reshape(row_count, seq_len, heads_here, HEAD_DIM)

    def self_backward(row_item):
        queries, key_heads, value_heads, log_total, d_context, segment_row = row_item
        return attend_backward(
            queries,
            key_heads,
            value_heads,
            log_total,
            d_context,
            causal_mask(segment_row),
            score_scale,
        )

    d_self_q, d_self_k, d_self_v = lax.map(
        self_backward, (self_q, self_k, self_v, self_lse, d_self_heads, tgt_segments)
    )
    d_mixed = jnp.stack((d_self_q, d_self_k, d_self_v), axis=2).reshape(
        row_count, seq_len, 3, 1, head_share
    )
    back_mixed = lax.all_to_all(d_mixed, "seq", split_axis=1, concat_axis=3, tiled=True).reshape(
        token_total, 3 * model_width
    )
    grad_qkv = left_dot(flat_tokens, back_mixed)
    grad_tokens = (d_resid_one + right_dot(back_mixed, w_qkv)).reshape(
        row_count, tok_local, model_width
    )
    summed = lax.psum(
        (
            grad_qkv,
            grad_self_out,
            grad_cross_q,
            grad_cross_kv,
            grad_cross_out,
            grad_up,
            grad_down,
            d_gain_one,
            d_bias_one,
            d_gain_two,
            d_bias_two,
            d_gain_three,
            d_bias_three,
        ),
        ("dp", "seq"),
    )
    return (
        output,
        grad_tokens,
        grad_memory,
        summed[0],
        summed[1],
        summed[2],
        summed[3],
        summed[4],
        summed[5],
        summed[6],
        summed[7],
        summed[8],
        summed[9],
        summed[10],
        summed[11],
        summed[12],
    )


def solution(mesh):
    return jax.shard_map(
        body,
        mesh=mesh,
        in_specs=(
            P("dp", "seq", None),
            P("dp", "seq", None),
            P("dp", None),
            P("dp", None),
            P("dp", "seq", None),
            P(),
            P(),
            P(),
            P(),
            P(),
            P(),
            P(),
            P(),
            P(),
            P(),
            P(),
            P(),
            P(),
        ),
        out_specs=(
            P("dp", "seq", None),
            P("dp", "seq", None),
            P("dp", "seq", None),
            P(),
            P(),
            P(),
            P(),
            P(),
            P(),
            P(),
            P(),
            P(),
            P(),
            P(),
            P(),
            P(),
        ),
        check_vma=False,
    )
```

profile of v0, /device:TPU:0, one launch (start us, length us, event | category | flops | bytes accessed | tf_op | source)
XLA Modules:
  0.0 717.0 jit_solution(7663693203559814328)
XLA Ops:
  7.2 3.8 convolution_convert_fusion
  11.0 3.9 reshape.401
  17.9 6.3 all-to-all-start
  24.2 37.1 %all-to-all-done = bf16[2,256,3,4,128]{4,1,2,0,3:T(8,128)(2,1)} async-done(((bf16[2,256,3,4,128]{4,1,2,0,3:T(8,128)(2,1)}), bf16[2,256,3,4,128]{4,1,2,0,3:T(8,128)(2,1)}, u32[]{:S(2)}, u32[]{:S(2)}) %all-to-all-start) | async-done | bytes 1572896 | tf_op jit(solution)/shard_map/all_to_all | solution.py:128
  61.3 3.8 copy.197
  65.0 3.8 reshape.402
  72.0 16.4 %while.52 = (s32[]{:T(128)}, bf16[2,1024,2,64]{1,3,2,0:T(8,128)(2,1)}, f32[2,2,1024,1]{2,1,3,0:T(2,128)S(1)}, bf16[2,1024,2,64]{1,3,2,0:T(8,128)(2,1)}, s32[2,10...) while((s32[]{:T(128)}, ...), condition=%wide.region_3.4_spmd, body=%wide.region_0.3_spmd.sunk | while | flops 565311488 | bytes 36780216 | solution.py:151
  90.7 4.1 all-to-all-start.1
  103.5 5.4 all-to-all-done.1
  108.9 4.3 all-to-all-start.2
  122.7 15.7 %all-to-all-done.2 = bf16[2,256,2,4,128]{4,2,1,0,3:T(2,128)(2,1)} async-done(((bf16[2,256,2,4,128]{4,2,1,0,3:T(2,128)(2,1)}), bf16[2,256,2,4,128]{4,2,1,0,3:T(2,128)(2,1)}, u32[]{:S(2)}, u32[]{:S(2)}) %all-to-all-start.2) | async-done | bytes 1048608 | tf_op jit(solution)/shard_map/all_to_all | solution.py:136
  138.4 4.4 all-to-all-start.3
  142.9 3.8 copy.202
  151.5 5.4 all-to-all-done.3
  162.1 18.5 %while.53 = (s32[]{:T(128)}, bf16[2,1024,2,64]{1,3,2,0:T(8,128)(2,1)}, f32[2,2,1024,1]{2,1,3,0:T(2,128)S(1)}, bf16[2,1024,2,64]{1,3,2,0:T(8,128)(2,1)}, s32[2,10...) while((s32[]{:T(128)}, ...), condition=%wide.region_9.10_spmd, body=%wide.region_6.9_spmd.sunk | while | flops 563214336 | bytes 36792512 | solution.py:180
  182.6 4.8 all-to-all-start.4
  189.4 12.1 %all-to-all-done.4 = bf16[2,1024,1,128]{3,0,2,1:T(2,128)(2,1)} async-done(((bf16[2,1024,1,128]{3,0,2,1:T(2,128)(2,1)}), bf16[2,1024,1,128]{3,0,2,1:T(2,128)(2,1)}, u32[]{:S(2)}, u32[]{:S(2)}) %all-to-all-start.4) | async-done | bytes 524320 | tf_op jit(solution)/shard_map/all_to_all | solution.py:183
  221.2 4.3 all-to-all-start.5
  225.5 14.1 %all-to-all-done.5 = bf16[2,256,4,128]{3,1,0,2:T(8,128)(2,1)} async-done(((bf16[2,256,4,128]{3,1,0,2:T(8,128)(2,1)}), bf16[2,256,4,128]{3,1,0,2:T(8,128)(2,1)}, u32[]{:S(2)}, u32[]{:S(2)}) %all-to-all-start.5) | async-done | bytes 524320 | tf_op jit(solution)/shard_map/all_to_all | solution.py:218
  246.6 27.1 %while.54 = (s32[]{:T(128)}, bf16[2,1024,2,64]{1,3,2,0:T(8,128)(2,1)}, bf16[2,1024,2,64]{1,3,2,0:T(8,128)(2,1)}, bf16[2,1024,2,64]{1,3,2,0:T(8,128)(2,1)}, bf16[...) while((s32[]{:T(128)}, ...), condition=%wide.region_20.21_spmd, body=%wide.region_18.20_spmd.sunk | while | flops 1375336448 | bytes 86594928 | solution.py:234
  275.1 16.4 %all_to_all.150 = bf16[2,1024,1,1,128]{4,0,3,2,1:T(2,128)(2,1)S(1)} all-to-all(bf16[2,1024,1,1,128]{4,0,3,2,1:T(2,128)(2,1)S(1)} %copy.210), channel_id=1, replica_groups=mesh['dp'=8,'seq'=4] {'seq'}, dimensions={1} | all-to-all | bytes 1048576 | tf_op jit(solution)/shard_map/all_to_all | solution.py:242
  296.0 4.1 all-to-all-start.7
  303.5 10.2 %all-to-all-done.7 = bf16[2,256,4,128]{3,1,0,2:T(8,128)(2,1)} async-done(((bf16[2,256,4,128]{3,1,0,2:T(8,128)(2,1)}), bf16[2,256,4,128]{3,1,0,2:T(8,128)(2,1)}, u32[]{:S(2)}, u32[]{:S(2)}) %all-to-all-start.7) | async-done | bytes 524320 | tf_op jit(solution)/shard_map/all_to_all | solution.py:265
  313.7 4.5 all-to-all-start.9
  323.4 27.0 %while.55 = (s32[]{:T(128)}, bf16[2,1024,2,64]{1,3,2,0:T(8,128)(2,1)}, bf16[2,1024,2,64]{1,3,2,0:T(8,128)(2,1)}, bf16[2,1024,2,64]{1,3,2,0:T(8,128)(2,1)}, bf16[...) while((s32[]{:T(128)}, ...), condition=%wide.region_25.26_spmd, body=%wide.region_23.25_spmd.sunk | while | flops 1377433600 | bytes 86582632 | solution.py:281
  353.2 5.0 copy.215
  358.2 5.1 all-to-all-start.8
  366.2 5.2 fusion.153
  383.1 16.2 %all-to-all-done.8 = bf16[2,1024,3,1,128]{4,0,3,2,1:T(2,128)(2,1)} async-done(((bf16[2,1024,3,1,128]{4,0,3,2,1:T(2,128)(2,1)}), bf16[2,1024,3,1,128]{4,0,3,2,1:T(2,128)(2,1)}, u32[]{:S(2)}, u32[]{:S(2)}) %all-to-all-start.8) | async-done | bytes 1572896 | tf_op jit(solution)/shard_map/all_to_all | solution.py:287
  409.5 40.1 %all-reduce = (f32[512]{0:T(512)}, f32[512]{0:T(512)}, f32[512]{0:T(512)}, f32[512]{0:T(512)}, f32[512]{0:T(512)}, /*index=5*/f32[512]{0:T(512)}) all-reduce(f32[512]{0:T(512)S(1)} %get-tuple-element.334, f32[512]{0:T(512)S(1)} %get-tuple-element.341, f32[512]{0:T(512)S(1)} %copy-done.74, ...), channel_id=1, replica_groups=mesh['dp'=8,'seq'=4] {'dp','seq'}, use_global_device_ids=true, to_apply=%region_34.35 | all-reduce | flops 3072 | bytes 24576 | tf_op jit(solution)/shard_map/psum | solution.py:294
  454.5 3.8 convolution_add_fusion.3
  458.3 234.8 %all-reduce.4.cloned.1.call-done = (f32[512,1536]{0,1:T(8,128)}, f32[512,512]{1,0:T(8,128)}, f32[512,512]{1,0:T(8,128)}, f32[512,1024]{0,1:T(8,128)}, f32[512,51...) async-done(((f32[512,1536]{0,1:T(8,128)}, f32[512,512]{1,0:T(8,128)}, f32[512,512]{1,0:T(8,128)}, f32[512,1024]{0,1:T(8,128)}, f32[512,512]{1,0:T(8,128)}, ...) | async-done | bytes 16777232 | tf_op jit(solution)/shard_map/psum | solution.py:294
  (357 shorter events, 218.6 us)
Async XLA Ops:
  7.2 198.6 %copy-start = (bf16[512,2048]{1,0:T(8,128)(2,1)S(1)}, bf16[512,2048]{1,0:T(8,128)(2,1)}, u32[]{:S(2)}) copy-start(bf16[512,2048]{1,0:T(8,128)(2,1)} %param.36) | copy-start | bytes 6291460
  17.9 43.4 %all-to-all-start = ((bf16[2,256,3,4,128]{4,1,2,0,3:T(8,128)(2,1)}), bf16[2,256,3,4,128]{4,1,2,0,3:T(8,128)(2,1)}, u32[]{:S(2)}, u32[]{:S(2)}) async-start(bf16[2,256,3,4,128]{4,1,2,0,3:T(8,128)(2,1)} %copy.196), calls=%async_computation | async-start | bytes 3145728 | tf_op jit(solution)/shard_map/all_to_all | solution.py:128
  88.4 15.1 %copy-start.5 = (bf16[2,1024,2,64]{1,3,2,0:T(8,128)(2,1)}, bf16[2,1024,2,64]{1,3,2,0:T(8,128)(2,1)S(1)}, u32[]{:S(2)}) copy-start(bf16[2,1024,2,64]{1,3,2,0:T(8,128)(2,1)S(1)} %get-tuple-element.855) | copy-start | bytes 1572868
  88.4 15.1 %copy-start.7 = (bf16[2,1024,2,64]{1,3,2,0:T(8,128)(2,1)}, bf16[2,1024,2,64]{1,3,2,0:T(8,128)(2,1)S(1)}, u32[]{:S(2)}) copy-start(bf16[2,1024,2,64]{1,3,2,0:T(8,128)(2,1)S(1)} %get-tuple-element.856) | copy-start | bytes 1572868
  88.4 15.1 %copy-start.59 = (f32[2,2,1024,1]{2,1,3,0:T(2,128)}, f32[2,2,1024,1]{2,1,3,0:T(2,128)S(1)}, u32[]{:S(2)}) copy-start(f32[2,2,1024,1]{2,1,3,0:T(2,128)S(1)} %get-tuple-element.796) | copy-start | bytes 49156
  90.7 18.2 %all-to-all-start.1 = ((bf16[2,1024,1,128]{3,0,2,1:T(2,128)(2,1)}), bf16[2,1024,1,128]{3,0,2,1:T(2,128)(2,1)}, u32[]{:S(2)}, u32[]{:S(2)}) async-start(bf16[2,1024,1,128]{3,0,2,1:T(2,128)(2,1)} %copy.198), calls=%async_computation.1 | async-start | bytes 1048576 | tf_op jit(solution)/shard_map/all_to_all | solution.py:152
  103.5 14.1 %copy-start.70 = (f32[512]{0:T(512)S(1)}, f32[512]{0:T(512)}, u32[]{:S(2)}) copy-start(f32[512]{0:T(512)} %param.38) | copy-start | bytes 6148
  103.5 14.1 %copy-start.76 = (f32[512]{0:T(512)S(1)}, f32[512]{0:T(512)}, u32[]{:S(2)}) copy-start(f32[512]{0:T(512)} %param.39) | copy-start | bytes 6148
  108.9 29.5 %all-to-all-start.2 = ((bf16[2,256,2,4,128]{4,2,1,0,3:T(2,128)(2,1)}), bf16[2,256,2,4,128]{4,2,1,0,3:T(2,128)(2,1)}, u32[]{:S(2)}, u32[]{:S(2)}) async-start(bf16[2,256,2,4,128]{4,2,1,0,3:T(2,128)(2,1)} %copy.201), calls=%async_computation.2 | async-start | bytes 2097152 | tf_op jit(solution)/shard_map/all_to_all | solution.py:136
  138.4 18.5 %all-to-all-start.3 = ((bf16[2,256,1,4,128]{4,1,0,2,3:T(8,128)(2,1)}), bf16[2,256,1,4,128]{4,1,0,2,3:T(8,128)(2,1)}, u32[]{:S(2)}, u32[]{:S(2)}) async-start(bf16[2,256,1,4,128]{4,1,0,2,3:T(8,128)(2,1)} %copy.203), calls=%async_computation.3 | async-start | bytes 1048576 | tf_op jit(solution)/shard_map/all_to_all | solution.py:170
  142.9 19.2 %copy-start.58 = (s32[2,1024]{1,0:T(2,128)S(1)}, s32[2,1024]{1,0:T(2,128)}, u32[]{:S(2)}) copy-start(s32[2,1024]{1,0:T(2,128)} %param.29) | copy-start | bytes 24580
  162.1 25.4 %copy-start.69 = (f32[512]{0:T(512)S(1)}, f32[512]{0:T(512)}, u32[]{:S(2)}) copy-start(f32[512]{0:T(512)} %param.42) | copy-start | bytes 6148
  182.6 23.2 %copy-start.65 = (f32[512]{0:T(512)S(1)}, f32[512]{0:T(512)}, u32[]{:S(2)}) copy-start(f32[512]{0:T(512)} %param.40) | copy-start | bytes 6148
  182.6 23.2 %copy-start.67 = (f32[512]{0:T(512)S(1)}, f32[512]{0:T(512)}, u32[]{:S(2)}) copy-start(f32[512]{0:T(512)} %param.41) | copy-start | bytes 6148
  182.6 18.9 %all-to-all-start.4 = ((bf16[2,1024,1,128]{3,0,2,1:T(2,128)(2,1)}), bf16[2,1024,1,128]{3,0,2,1:T(2,128)(2,1)}, u32[]{:S(2)}, u32[]{:S(2)}) async-start(bf16[2,1024,1,128]{3,0,2,1:T(2,128)(2,1)} %copy.205), calls=%async_computation.4 | async-start | bytes 1048576 | tf_op jit(solution)/shard_map/all_to_all | solution.py:183
  216.0 29.8 %copy-start.10 = (f32[512,512]{1,0:T(8,128)}, f32[512,512]{1,0:T(8,128)S(1)}, u32[]{:S(2)}) copy-start(f32[512,512]{1,0:T(8,128)S(1)} %subtract_multiply_fusion.1) | copy-start | bytes 3145732
  216.0 30.6 %copy-start.4 = (bf16[2,1024,2,64]{1,3,2,0:T(8,128)(2,1)S(1)}, bf16[2,1024,2,64]{1,3,2,0:T(8,128)(2,1)}, u32[]{:S(2)}) copy-start(bf16[2,1024,2,64]{1,3,2,0:T(8,128)(2,1)} %get-tuple-element.854) | copy-start | bytes 1572868
  216.0 30.6 %copy-start.9 = (bf16[2,1024,2,64]{1,3,2,0:T(8,128)(2,1)S(1)}, bf16[2,1024,2,64]{1,3,2,0:T(8,128)(2,1)}, u32[]{:S(2)}) copy-start(bf16[2,1024,2,64]{1,3,2,0:T(8,128)(2,1)} %get-tuple-element.857) | copy-start | bytes 1572868
  221.2 18.4 %all-to-all-start.5 = ((bf16[2,256,4,128]{3,1,0,2:T(8,128)(2,1)}), bf16[2,256,4,128]{3,1,0,2:T(8,128)(2,1)}, u32[]{:S(2)}, u32[]{:S(2)}) async-start(bf16[2,256,4,128]{3,1,0,2:T(8,128)(2,1)} %copy.208), calls=%async_computation.5 | async-start | bytes 1048576 | tf_op jit(solution)/shard_map/all_to_all | solution.py:218
  273.7 18.3 %copy-start.11 = (f32[512,512]{1,0:T(8,128)S(1)}, f32[512,512]{1,0:T(8,128)}, u32[]{:S(2)}) copy-start(f32[512,512]{1,0:T(8,128)} %copy-done.10) | copy-start | bytes 3145732
  296.0 17.8 %all-to-all-start.7 = ((bf16[2,256,4,128]{3,1,0,2:T(8,128)(2,1)}), bf16[2,256,4,128]{3,1,0,2:T(8,128)(2,1)}, u32[]{:S(2)}, u32[]{:S(2)}) async-start(bf16[2,256,4,128]{3,1,0,2:T(8,128)(2,1)} %copy.213), calls=%async_computation.7 | async-start | bytes 1048576 | tf_op jit(solution)/shard_map/all_to_all | solution.py:265
  301.4 21.9 %copy-start.6 = (bf16[2,1024,2,64]{1,3,2,0:T(8,128)(2,1)S(1)}, bf16[2,1024,2,64]{1,3,2,0:T(8,128)(2,1)}, u32[]{:S(2)}) copy-start(bf16[2,1024,2,64]{1,3,2,0:T(8,128)(2,1)} %copy-done.5) | copy-start | bytes 1572868
  301.4 21.9 %copy-start.8 = (bf16[2,1024,2,64]{1,3,2,0:T(8,128)(2,1)S(1)}, bf16[2,1024,2,64]{1,3,2,0:T(8,128)(2,1)}, u32[]{:S(2)}) copy-start(bf16[2,1024,2,64]{1,3,2,0:T(8,128)(2,1)} %copy-done.7) | copy-start | bytes 1572868
  301.5 21.9 %copy-start.60 = (f32[2,2,1024,1]{2,1,3,0:T(2,128)S(1)}, f32[2,2,1024,1]{2,1,3,0:T(2,128)}, u32[]{:S(2)}) copy-start(f32[2,2,1024,1]{2,1,3,0:T(2,128)} %copy-done.59) | copy-start | bytes 49156
  313.7 44.5 %all-to-all-start.9 = ((bf16[2,1024,2,1,128]{4,0,3,2,1:T(2,128)(2,1)}), bf16[2,1024,2,1,128]{4,0,3,2,1:T(2,128)(2,1)}, u32[]{:S(2)}, u32[]{:S(2)}) async-start(bf16[2,1024,2,1,128]{4,0,3,2,1:T(2,128)(2,1)} %copy.218), calls=%async_computation.9 | async-start | bytes 2097152 | tf_op jit(solution)/shard_map/all_to_all | solution.py:249
  350.4 13.3 %copy-start.12 = (f32[512,512]{1,0:T(8,128)S(1)}, f32[512,512]{1,0:T(8,128)}, u32[]{:S(2)}) copy-start(f32[512,512]{1,0:T(8,128)} %copy-done.10) | copy-start | bytes 3145732
  353.2 13.0 %copy-start.64 = (f32[512]{0:T(512)S(1)}, f32[512]{0:T(512)}, u32[]{:S(2)}) copy-start(f32[512]{0:T(512)} %copy-done.63) | copy-start | bytes 6148
  353.2 13.0 %copy-start.66 = (f32[512]{0:T(512)S(1)}, f32[512]{0:T(512)}, u32[]{:S(2)}) copy-start(f32[512]{0:T(512)} %param.40) | copy-start | bytes 6148
  353.2 13.0 %copy-start.68 = (f32[512]{0:T(512)S(1)}, f32[512]{0:T(512)}, u32[]{:S(2)}) copy-start(f32[512]{0:T(512)} %param.41) | copy-start | bytes 6148
  358.2 41.1 %all-to-all-start.8 = ((bf16[2,1024,3,1,128]{4,0,3,2,1:T(2,128)(2,1)}), bf16[2,1024,3,1,128]{4,0,3,2,1:T(2,128)(2,1)}, u32[]{:S(2)}, u32[]{:S(2)}) async-start(bf16[2,1024,3,1,128]{4,0,3,2,1:T(2,128)(2,1)} %copy.215), calls=%async_computation.8 | async-start | bytes 3145728 | tf_op jit(solution)/shard_map/all_to_all | solution.py:287
  363.3 329.8 %all-reduce.4.cloned.1.call-start = ((), (), s32[]{:S(2)}) async-start(), calls=%async_computation.10 | async-start | bytes 33554432 | tf_op jit(solution)/shard_map/psum | solution.py:294
  383.1 23.1 %copy-start.51 = (bf16[2,256,512]{2,1,0:T(8,128)(2,1)S(1)}, bf16[2,256,512]{2,1,0:T(8,128)(2,1)}, u32[]{:S(2)}) copy-start(bf16[2,256,512]{2,1,0:T(8,128)(2,1)} %param.26) | copy-start | bytes 1572868
  (79 other events, 247.0 us)
Sparse Core Ops, SparseCore 0:
  409.0 284.0 all-reduce.3
where the time goes:
time: 728 us; the launch traced here: 717 us
  waiting for transfers between devices  351 us (48%)
  local copies, waits for them, and re-layouts  112 us (15%)
  matrix products  105 us (14%)
  blocking collectives  56.5 us (8%)
  starting transfers between devices  42.4 us (6%)
  other arithmetic  33.6 us (5%)
  between operations  14.9 us (2%)
    psum x1, waiting for transfers between devices, body(): lax.psum((grad_qkv, grad_self_out, grad_cross_q, grad_cross_kv, grad_cros...  235 us
    psum x1, blocking collectives, body(): lax.psum((grad_qkv, grad_self_out, grad_cross_q, grad_cross_kv, grad_cros...  40.1 us
    all_to_all x1, waiting for transfers between devices, body(): lax.all_to_all(mixed_proj, 'seq', split_axis=3, concat_axis=1, tiled=True)  37.1 us
    unnamed x122, local copies, waits for them, and re-layouts  19.7 us
    dot_general x7, matrix products, left_dot(): lax.dot_general(left, right, (((0,), (0,)), ((), ())), preferred_element_...  19 us
    all_to_all x1, blocking collectives, body(): lax.all_to_all(d_cross_q.reshape(row_count, seq_len, 1, 1, head_share), '...  16.4 us
    all_to_all x1, waiting for transfers between devices, body(): lax.all_to_all(d_mixed, 'seq', split_axis=1, concat_axis=3, tiled=True)  16.2 us
    all_to_all x1, waiting for transfers between devices, body(): lax.all_to_all(memory_proj, 'seq', split_axis=3, concat_axis=1, tiled=True)  15.7 us
  transfers between devices with their start and end apart: 10, of which 9 were waited for; matrix products, arithmetic and copies ran while one was open for 14% of the time, Pallas kernels for 0%

commit v1 on v0

--- a/solution.py
+++ b/solution.py
@@ -292,22 +292,25 @@
         row_count, tok_local, model_width
     )
     summed = lax.psum(
-        (
-            grad_qkv,
-            grad_self_out,
-            grad_cross_q,
-            grad_cross_kv,
-            grad_cross_out,
-            grad_up,
-            grad_down,
-            d_gain_one,
-            d_bias_one,
-            d_gain_two,
-            d_bias_two,
-            d_gain_three,
-            d_bias_three,
+        lax.psum(
+            (
+                grad_qkv,
+                grad_self_out,
+                grad_cross_q,
+                grad_cross_kv,
+                grad_cross_out,
+                grad_up,
+                grad_down,
+                d_gain_one,
+                d_bias_one,
+                d_gain_two,
+                d_bias_two,
+                d_gain_three,
+                d_bias_three,
+            ),
+            "seq",
         ),
-        ("dp", "seq"),
+        "dp",
     )
     return (
         output,

time: 728 us -> 1240 us (1.70)
  waiting for transfers between devices: 351 us -> 861 us
    psum x1, waiting for transfers between devices: 235 us -> 568 us  [body(): lax.psum((grad_qkv, grad_self_out, grad_cross_q, grad_cross_kv, grad_cros...]
    psum x0 -> x1, waiting for transfers between devices: none -> 176 us  [body(): lax.psum(lax.psum((grad_qkv, grad_self_out, grad_cross_q, grad_cross_kv,...]
    psum x0 -> x1, blocking collectives: none -> 24.1 us  [body(): lax.psum(lax.psum((grad_qkv, grad_self_out, grad_cross_q, grad_cross_kv,...]
    psum x1, blocking collectives: 40.1 us -> 16 us  [body(): lax.psum((grad_qkv, grad_self_out, grad_cross_q, grad_cross_kv, grad_cros...]
  transfers between devices with their start and end apart: 10 -> 11, of which waited for: 9 -> 10; matrix products, arithmetic and copies ran while one was open for 14% -> 8% of each run, Pallas kernels for 0% -> 0%
where the time goes in v1:
time: 1240 us; the launch traced here: 1230 us
  waiting for transfers between devices  861 us (69%)
  local copies, waits for them, and re-layouts  110 us (9%)
  matrix products  108 us (9%)
  blocking collectives  56.5 us (5%)
  starting transfers between devices  42.3 us (3%)
  other arithmetic  33.6 us (3%)
  between operations  14.9 us (1%)
    psum x1, waiting for transfers between devices, body(): lax.psum((grad_qkv, grad_self_out, grad_cross_q, grad_cross_kv, grad_cros...  568 us
    psum x1, waiting for transfers between devices, body(): lax.psum(lax.psum((grad_qkv, grad_self_out, grad_cross_q, grad_cross_kv,...  176 us
    all_to_all x1, waiting for transfers between devices, body(): lax.all_to_all(mixed_proj, 'seq', split_axis=3, concat_axis=1, tiled=True)  37.1 us
  transfers between devices with their start and end apart: 11, of which 10 were waited for; matrix products, arithmetic and copies ran while one was open for 8% of the time, Pallas kernels for 0%

profile of v1, /device:TPU:0, one launch (start us, length us, event | category | flops | bytes accessed | tf_op | source)
XLA Modules:
  0.0 1227.7 jit_solution(15992454373807563648)
XLA Ops:
  7.2 3.8 convolution_convert_fusion
  11.0 3.9 reshape.401
  17.9 6.3 all-to-all-start
  24.2 37.1 %all-to-all-done = bf16[2,256,3,4,128]{4,1,2,0,3:T(8,128)(2,1)} async-done(((bf16[2,256,3,4,128]{4,1,2,0,3:T(8,128)(2,1)}), bf16[2,256,3,4,128]{4,1,2,0,3:T(8,128)(2,1)}, u32[]{:S(2)}, u32[]{:S(2)}) %all-to-all-start) | async-done | bytes 1572896 | tf_op jit(solution)/shard_map/all_to_all | solution.py:128
  65.0 3.8 reshape.402
  72.2 18.4 %while.52 = (s32[]{:T(128)}, bf16[2,1024,2,64]{1,3,2,0:T(8,128)(2,1)}, f32[2,2,1024,1]{2,1,3,0:T(2,128)S(1)}, bf16[2,1024,2,64]{1,3,2,0:T(8,128)(2,1)}, s32[2,10...) while((s32[]{:T(128)}, ...), condition=%wide.region_3.4_spmd, body=%wide.region_0.3_spmd.sunk | while | flops 565311488 | bytes 36780216 | solution.py:151
  92.6 4.1 all-to-all-start.1
  103.4 7.4 all-to-all-done.1
  110.8 4.2 all-to-all-start.2
  125.6 14.7 %all-to-all-done.2 = bf16[2,256,2,4,128]{4,2,1,0,3:T(2,128)(2,1)} async-done(((bf16[2,256,2,4,128]{4,2,1,0,3:T(2,128)(2,1)}), bf16[2,256,2,4,128]{4,2,1,0,3:T(2,128)(2,1)}, u32[]{:S(2)}, u32[]{:S(2)}) %all-to-all-start.2) | async-done | bytes 1048608 | tf_op jit(solution)/shard_map/all_to_all | solution.py:136
  140.4 4.4 all-to-all-start.3
  144.8 3.8 copy.202
  153.5 5.4 all-to-all-done.3
  164.0 18.5 %while.53 = (s32[]{:T(128)}, bf16[2,1024,2,64]{1,3,2,0:T(8,128)(2,1)}, f32[2,2,1024,1]{2,1,3,0:T(2,128)S(1)}, bf16[2,1024,2,64]{1,3,2,0:T(8,128)(2,1)}, s32[2,10...) while((s32[]{:T(128)}, ...), condition=%wide.region_9.10_spmd, body=%wide.region_6.9_spmd.sunk | while | flops 563214336 | bytes 36792512 | solution.py:180
  184.5 4.8 all-to-all-start.4
  191.3 12.1 all-to-all-done.4
  223.0 4.3 all-to-all-start.5
  227.4 14.0 %all-to-all-done.5 = bf16[2,256,4,128]{3,1,0,2:T(8,128)(2,1)} async-done(((bf16[2,256,4,128]{3,1,0,2:T(8,128)(2,1)}), bf16[2,256,4,128]{3,1,0,2:T(8,128)(2,1)}, u32[]{:S(2)}, u32[]{:S(2)}) %all-to-all-start.5) | async-done | bytes 524320 | tf_op jit(solution)/shard_map/all_to_all | solution.py:218
  248.3 27.1 %while.54 = (s32[]{:T(128)}, bf16[2,1024,2,64]{1,3,2,0:T(8,128)(2,1)}, bf16[2,1024,2,64]{1,3,2,0:T(8,128)(2,1)}, bf16[2,1024,2,64]{1,3,2,0:T(8,128)(2,1)}, bf16[...) while((s32[]{:T(128)}, ...), condition=%wide.region_20.21_spmd, body=%wide.region_18.20_spmd.sunk | while | flops 1375336448 | bytes 86594928 | solution.py:234
  276.8 16.4 %all_to_all.150 = bf16[2,1024,1,1,128]{4,0,3,2,1:T(2,128)(2,1)S(1)} all-to-all(bf16[2,1024,1,1,128]{4,0,3,2,1:T(2,128)(2,1)S(1)} %copy.210), channel_id=1, replica_groups=mesh['dp'=8,'seq'=4] {'seq'}, dimensions={1} | all-to-all | bytes 1048576 | tf_op jit(solution)/shard_map/all_to_all | solution.py:242
  297.7 4.1 all-to-all-start.7
  305.2 10.2 all-to-all-done.7
  315.4 4.5 all-to-all-start.9
  325.0 27.0 %while.55 = (s32[]{:T(128)}, bf16[2,1024,2,64]{1,3,2,0:T(8,128)(2,1)}, bf16[2,1024,2,64]{1,3,2,0:T(8,128)(2,1)}, bf16[2,1024,2,64]{1,3,2,0:T(8,128)(2,1)}, bf16[...) while((s32[]{:T(128)}, ...), condition=%wide.region_25.26_spmd, body=%wide.region_23.25_spmd.sunk | while | flops 1377433600 | bytes 86582632 | solution.py:281
  354.8 5.0 copy.215
  359.9 5.1 all-to-all-start.8
  367.9 5.2 fusion.153
  384.7 16.3 %all-to-all-done.8 = bf16[2,1024,3,1,128]{4,0,3,2,1:T(2,128)(2,1)} async-done(((bf16[2,1024,3,1,128]{4,0,3,2,1:T(2,128)(2,1)}), bf16[2,1024,3,1,128]{4,0,3,2,1:T(2,128)(2,1)}, u32[]{:S(2)}, u32[]{:S(2)}) %all-to-all-start.8) | async-done | bytes 1572896 | tf_op jit(solution)/shard_map/all_to_all | solution.py:287
  410.5 567.6 %all-reduce.9.cloned.1.call-done = (f32[512,1536]{0,1:T(8,128)}, f32[512,512]{1,0:T(8,128)}, f32[512,512]{1,0:T(8,128)}, f32[512,1024]{0,1:T(8,128)}, f32[512,51...) async-done(((f32[512,1536]{0,1:T(8,128)}, f32[512,512]{1,0:T(8,128)}, f32[512,512]{1,0:T(8,128)}, f32[512,1024]{0,1:T(8,128)}, f32[512,512]{1,0:T(8,128)}, ...) | async-done | bytes 16777232 | tf_op jit(solution)/shard_map/psum | solution.py:295
  978.9 16.0 %all-reduce.2 = (f32[512]{0:T(512)S(1)}, f32[512]{0:T(512)S(1)}, f32[512]{0:T(512)S(1)}, f32[512]{0:T(512)S(1)}, f32[512]{0:T(512)S(1)}, /*index=5*/f32[512]{0:T(512)S(1)}) all-reduce(f32[512]{0:T(512)S(1)} %get-tuple-element.334, f32[512]{0:T(512)S(1)} %get-tuple-element.341, ...), channel_id=1, replica_groups=mesh['dp'=8,'seq'=4] {'seq'}, use_global_device_ids=true, to_apply=%region_41.42 | all-reduce | flops 3072 | bytes 24576 | tf_op jit(solution)/shard_map/psum | solution.py:295
  994.9 24.1 %all-reduce = (f32[512]{0:T(512)}, f32[512]{0:T(512)}, f32[512]{0:T(512)}, f32[512]{0:T(512)}, f32[512]{0:T(512)}, /*index=5*/f32[512]{0:T(512)}) all-reduce(f32[512]{0:T(512)S(1)} %get-tuple-element.429, f32[512]{0:T(512)S(1)} %get-tuple-element.430, f32[512]{0:T(512)S(1)} %get-tuple-element.431, ...), channel_id=1, replica_groups=mesh['dp'=8,'seq'=4] {'dp'}, use_global_device_ids=true, to_apply=%region_42.43 | all-reduce | flops 3072 | bytes 24576 | tf_op jit(solution)/shard_map/psum | solution.py:294
  1027.6 176.3 %all-reduce.7.cloned.1.call-done = (f32[512,1536]{0,1:T(8,128)}, f32[512,512]{1,0:T(8,128)}, f32[512,512]{1,0:T(8,128)}, f32[512,1024]{0,1:T(8,128)}, f32[512,51...) async-done(((f32[512,1536]{0,1:T(8,128)}, f32[512,512]{1,0:T(8,128)}, f32[512,512]{1,0:T(8,128)}, f32[512,1024]{0,1:T(8,128)}, f32[512,512]{1,0:T(8,128)}, ...) | async-done | bytes 16777232 | tf_op jit(solution)/shard_map/psum | solution.py:294
  (355 shorter events, 226.8 us)
Async XLA Ops:
  7.2 200.5 %copy-start = (bf16[512,2048]{1,0:T(8,128)(2,1)S(1)}, bf16[512,2048]{1,0:T(8,128)(2,1)}, u32[]{:S(2)}) copy-start(bf16[512,2048]{1,0:T(8,128)(2,1)} %param.36) | copy-start | bytes 6291460
  17.9 43.4 %all-to-all-start = ((bf16[2,256,3,4,128]{4,1,2,0,3:T(8,128)(2,1)}), bf16[2,256,3,4,128]{4,1,2,0,3:T(8,128)(2,1)}, u32[]{:S(2)}, u32[]{:S(2)}) async-start(bf16[2,256,3,4,128]{4,1,2,0,3:T(8,128)(2,1)} %copy.196), calls=%async_computation | async-start | bytes 3145728 | tf_op jit(solution)/shard_map/all_to_all | solution.py:128
  92.6 18.2 %all-to-all-start.1 = ((bf16[2,1024,1,128]{3,0,2,1:T(2,128)(2,1)}), bf16[2,1024,1,128]{3,0,2,1:T(2,128)(2,1)}, u32[]{:S(2)}, u32[]{:S(2)}) async-start(bf16[2,1024,1,128]{3,0,2,1:T(2,128)(2,1)} %copy.198), calls=%async_computation.1 | async-start | bytes 1048576 | tf_op jit(solution)/shard_map/all_to_all | solution.py:152
  103.4 16.0 %copy-start.67 = (f32[512]{0:T(512)S(1)}, f32[512]{0:T(512)}, u32[]{:S(2)}) copy-start(f32[512]{0:T(512)} %param.38) | copy-start | bytes 6148
  103.4 16.0 %copy-start.73 = (f32[512]{0:T(512)S(1)}, f32[512]{0:T(512)}, u32[]{:S(2)}) copy-start(f32[512]{0:T(512)} %param.39) | copy-start | bytes 6148
  110.8 29.5 %all-to-all-start.2 = ((bf16[2,256,2,4,128]{4,2,1,0,3:T(2,128)(2,1)}), bf16[2,256,2,4,128]{4,2,1,0,3:T(2,128)(2,1)}, u32[]{:S(2)}, u32[]{:S(2)}) async-start(bf16[2,256,2,4,128]{4,2,1,0,3:T(2,128)(2,1)} %copy.201), calls=%async_computation.2 | async-start | bytes 2097152 | tf_op jit(solution)/shard_map/all_to_all | solution.py:136
  140.4 18.5 %all-to-all-start.3 = ((bf16[2,256,1,4,128]{4,1,0,2,3:T(8,128)(2,1)}), bf16[2,256,1,4,128]{4,1,0,2,3:T(8,128)(2,1)}, u32[]{:S(2)}, u32[]{:S(2)}) async-start(bf16[2,256,1,4,128]{4,1,0,2,3:T(8,128)(2,1)} %copy.203), calls=%async_computation.3 | async-start | bytes 1048576 | tf_op jit(solution)/shard_map/all_to_all | solution.py:170
  144.8 19.2 %copy-start.55 = (s32[2,1024]{1,0:T(2,128)S(1)}, s32[2,1024]{1,0:T(2,128)}, u32[]{:S(2)}) copy-start(s32[2,1024]{1,0:T(2,128)} %param.29) | copy-start | bytes 24580
  164.0 25.3 %copy-start.66 = (f32[512]{0:T(512)S(1)}, f32[512]{0:T(512)}, u32[]{:S(2)}) copy-start(f32[512]{0:T(512)} %param.42) | copy-start | bytes 6148
  184.5 23.1 %copy-start.62 = (f32[512]{0:T(512)S(1)}, f32[512]{0:T(512)}, u32[]{:S(2)}) copy-start(f32[512]{0:T(512)} %param.40) | copy-start | bytes 6148
  184.5 23.1 %copy-start.64 = (f32[512]{0:T(512)S(1)}, f32[512]{0:T(512)}, u32[]{:S(2)}) copy-start(f32[512]{0:T(512)} %param.41) | copy-start | bytes 6148
  184.5 18.8 %all-to-all-start.4 = ((bf16[2,1024,1,128]{3,0,2,1:T(2,128)(2,1)}), bf16[2,1024,1,128]{3,0,2,1:T(2,128)(2,1)}, u32[]{:S(2)}, u32[]{:S(2)}) async-start(bf16[2,1024,1,128]{3,0,2,1:T(2,128)(2,1)} %copy.205), calls=%async_computation.4 | async-start | bytes 1048576 | tf_op jit(solution)/shard_map/all_to_all | solution.py:183
  217.9 29.5 %copy-start.8 = (f32[512,512]{1,0:T(8,128)}, f32[512,512]{1,0:T(8,128)S(1)}, u32[]{:S(2)}) copy-start(f32[512,512]{1,0:T(8,128)S(1)} %subtract_multiply_fusion.1) | copy-start | bytes 3145732
  217.9 30.4 %copy-start.4 = (bf16[2,1024,2,64]{1,3,2,0:T(8,128)(2,1)S(1)}, bf16[2,1024,2,64]{1,3,2,0:T(8,128)(2,1)}, u32[]{:S(2)}) copy-start(bf16[2,1024,2,64]{1,3,2,0:T(8,128)(2,1)} %get-tuple-element.881) | copy-start | bytes 1572868
  217.9 30.4 %copy-start.7 = (bf16[2,1024,2,64]{1,3,2,0:T(8,128)(2,1)S(1)}, bf16[2,1024,2,64]{1,3,2,0:T(8,128)(2,1)}, u32[]{:S(2)}) copy-start(bf16[2,1024,2,64]{1,3,2,0:T(8,128)(2,1)} %get-tuple-element.884) | copy-start | bytes 1572868
  223.0 18.4 %all-to-all-start.5 = ((bf16[2,256,4,128]{3,1,0,2:T(8,128)(2,1)}), bf16[2,256,4,128]{3,1,0,2:T(8,128)(2,1)}, u32[]{:S(2)}, u32[]{:S(2)}) async-start(bf16[2,256,4,128]{3,1,0,2:T(8,128)(2,1)} %copy.208), calls=%async_computation.5 | async-start | bytes 1048576 | tf_op jit(solution)/shard_map/all_to_all | solution.py:218
  275.4 18.3 %copy-start.9 = (f32[512,512]{1,0:T(8,128)S(1)}, f32[512,512]{1,0:T(8,128)}, u32[]{:S(2)}) copy-start(f32[512,512]{1,0:T(8,128)} %copy-done.8) | copy-start | bytes 3145732
  297.7 17.8 %all-to-all-start.7 = ((bf16[2,256,4,128]{3,1,0,2:T(8,128)(2,1)}), bf16[2,256,4,128]{3,1,0,2:T(8,128)(2,1)}, u32[]{:S(2)}, u32[]{:S(2)}) async-start(bf16[2,256,4,128]{3,1,0,2:T(8,128)(2,1)} %copy.213), calls=%async_computation.7 | async-start | bytes 1048576 | tf_op jit(solution)/shard_map/all_to_all | solution.py:265
  303.1 21.9 %copy-start.5 = (bf16[2,1024,2,64]{1,3,2,0:T(8,128)(2,1)S(1)}, bf16[2,1024,2,64]{1,3,2,0:T(8,128)(2,1)}, u32[]{:S(2)}) copy-start(bf16[2,1024,2,64]{1,3,2,0:T(8,128)(2,1)} %get-tuple-element.882) | copy-start | bytes 1572868
  303.1 21.9 %copy-start.6 = (bf16[2,1024,2,64]{1,3,2,0:T(8,128)(2,1)S(1)}, bf16[2,1024,2,64]{1,3,2,0:T(8,128)(2,1)}, u32[]{:S(2)}) copy-start(bf16[2,1024,2,64]{1,3,2,0:T(8,128)(2,1)} %get-tuple-element.883) | copy-start | bytes 1572868
  303.1 21.8 %copy-start.57 = (f32[2,2,1024,1]{2,1,3,0:T(2,128)S(1)}, f32[2,2,1024,1]{2,1,3,0:T(2,128)}, u32[]{:S(2)}) copy-start(f32[2,2,1024,1]{2,1,3,0:T(2,128)} %copy-done.56) | copy-start | bytes 49156
  315.4 44.4 %all-to-all-start.9 = ((bf16[2,1024,2,1,128]{4,0,3,2,1:T(2,128)(2,1)}), bf16[2,1024,2,1,128]{4,0,3,2,1:T(2,128)(2,1)}, u32[]{:S(2)}, u32[]{:S(2)}) async-start(bf16[2,1024,2,1,128]{4,0,3,2,1:T(2,128)(2,1)} %copy.218), calls=%async_computation.9 | async-start | bytes 2097152 | tf_op jit(solution)/shard_map/all_to_all | solution.py:249
  352.0 13.3 %copy-start.10 = (f32[512,512]{1,0:T(8,128)S(1)}, f32[512,512]{1,0:T(8,128)}, u32[]{:S(2)}) copy-start(f32[512,512]{1,0:T(8,128)} %copy-done.8) | copy-start | bytes 3145732
  354.8 13.0 %copy-start.3 = (f32[512,512]{1,0:T(8,128)S(1)}, f32[512,512]{1,0:T(8,128)}, u32[]{:S(2)}) copy-start(f32[512,512]{1,0:T(8,128)} %copy-done.2) | copy-start | bytes 3145732
  354.8 13.0 %copy-start.59 = (f32[512]{0:T(512)S(1)}, f32[512]{0:T(512)}, u32[]{:S(2)}) copy-start(f32[512]{0:T(512)} %copy-done.58) | copy-start | bytes 6148
  354.8 13.0 %copy-start.61 = (f32[512]{0:T(512)S(1)}, f32[512]{0:T(512)}, u32[]{:S(2)}) copy-start(f32[512]{0:T(512)} %copy-done.60) | copy-start | bytes 6148
  354.8 13.0 %copy-start.63 = (f32[512]{0:T(512)S(1)}, f32[512]{0:T(512)}, u32[]{:S(2)}) copy-start(f32[512]{0:T(512)} %param.40) | copy-start | bytes 6148
  354.8 13.0 %copy-start.65 = (f32[512]{0:T(512)S(1)}, f32[512]{0:T(512)}, u32[]{:S(2)}) copy-start(f32[512]{0:T(512)} %param.41) | copy-start | bytes 6148
  359.9 41.1 %all-to-all-start.8 = ((bf16[2,1024,3,1,128]{4,0,3,2,1:T(2,128)(2,1)}), bf16[2,1024,3,1,128]{4,0,3,2,1:T(2,128)(2,1)}, u32[]{:S(2)}, u32[]{:S(2)}) async-start(bf16[2,1024,3,1,128]{4,0,3,2,1:T(2,128)(2,1)} %copy.215), calls=%async_computation.8 | async-start | bytes 3145728 | tf_op jit(solution)/shard_map/all_to_all | solution.py:287
  364.9 613.2 %all-reduce.9.cloned.1.call-start = ((), (), s32[]{:S(2)}) async-start(), calls=%async_computation.11 | async-start | bytes 33554432 | tf_op jit(solution)/shard_map/psum | solution.py:295
  384.7 23.1 %copy-start.49 = (bf16[2,256,512]{2,1,0:T(8,128)(2,1)S(1)}, bf16[2,256,512]{2,1,0:T(8,128)(2,1)}, u32[]{:S(2)}) copy-start(bf16[2,256,512]{2,1,0:T(8,128)(2,1)} %param.26) | copy-start | bytes 1572868
  410.5 793.3 %all-reduce.7.cloned.1.call-start = ((), (), s32[]{:S(2)}) async-start(), calls=%async_computation.10 | async-start | bytes 33554432 | tf_op jit(solution)/shard_map/psum | solution.py:294
  (77 other events, 229.5 us)
Sparse Core Ops, SparseCore 0:
  410.6 567.5 all-reduce.8
  983.3 220.4 all-reduce.6
